TPU v7x, 32 devices: a whole 2x2x4 slice. The times are simulated.
32 devices in a mesh: groups: 2 (over y), expert: 8 (over z, x), hidden: 2 (over core).
Axes of the slice: x: 2, y: 2, z: 4, core: 2. Of those that a mesh axis runs over, the one named last changes fastest.
Arguments:
- tokens: bfloat16 [128, 3072], P(('groups', 'expert'), 'hidden'), parts along dimension 0, may hold values from -6 to 6
- expert_ids: int32 [128, 4], P(('groups', 'expert')), parts along dimension 0, may hold values from 0 to 15, all different within a row; in each aligned block of 8 rows (0 to 7, 8 to 15, ...) at most 4 rows name the same one
- gate_codes: int32 [128, 4], P(('groups', 'expert')), parts along dimension 0, may hold values from 1 to 65535
- gate_weight: bfloat16 [8, 5376, 3072], P('expert', 'hidden'), may hold values from -0.109375 to 0.109375
- up_weight: bfloat16 [8, 5376, 3072], P('expert', 'hidden'), may hold values from -0.109375 to 0.109375
- down_weight: bfloat16 [8, 5376, 3072], P('expert', 'hidden'), may hold values from -0.078125 to 0.078125
Outputs:
- mixed: bfloat16 [128, 3072], P(('groups', 'expert'), 'hidden'), parts along dimension 0
There are 2 independent parts, one for each index of `groups`. A program takes and returns all parts, laid end to end along the dimension named above; an argument that names none is the same for every part. Nothing has to cross between parts.
Inputs may be any that keep to these rules, and one draw needn't show every extreme that they name: `expert_ids`: each token names 4 different experts; experts numbered 8 or more are held elsewhere and add nothing here; the 8 tokens of one device name one expert at most 4 times, a bound that some block reaches.
All inputs are finite; a program needn't handle non-finite values.
Results may differ from a plain program's by a relative error of at most 0.009.
Values may be sent and summed in bfloat16 or wider, within the bound.
A program may use at most 128 MiB of HBM per device.

v0:
```python
import jax
import jax.numpy as jnp
from jax import lax
from jax.sharding import PartitionSpec as P

EXPERTS = 8
CAP = 4


def per_device(tokens, expert_ids, gate_codes, gate_weight, up_weight, down_weight):
    tok_dev = tokens.shape[0]
    expert_count = lax.axis_size("expert")
    slices = expert_count // EXPERTS
    flat_ids = expert_ids.reshape(-1)
    route_count = flat_ids.shape[0]
    top_count = expert_ids.shape[1]
    onehot = (flat_ids[:, None] == jnp.arange(EXPERTS, dtype=jnp.int32)[None, :]).astype(jnp.int32)
    position = jnp.sum((jnp.cumsum(onehot, axis=0) - onehot) * onehot, axis=1)
    target = jnp.where(flat_ids < EXPERTS, flat_ids * CAP + position, -1)
    slot_hit = (target[:, None] == jnp.arange(EXPERTS * CAP, dtype=jnp.int32)[None, :]).astype(
        jnp.float32
    )
    token_of = jnp.arange(route_count, dtype=jnp.int32) // top_count
    owner_hit = (token_of[:, None] == jnp.arange(tok_dev, dtype=jnp.int32)[None, :]).astype(
        jnp.float32
    )
    gate_values = gate_codes.reshape(-1).astype(jnp.float32) / 32768.0
    dispatch = jnp.dot(slot_hit.T, owner_hit, precision=lax.Precision.HIGHEST).astype(jnp.bfloat16)
    weighted = jnp.dot(
        slot_hit.T, owner_hit * gate_values[:, None], precision=lax.Precision.HIGHEST
    )
    counts = jnp.sum(onehot, axis=0).astype(jnp.bfloat16)
    count_send = jnp.broadcast_to(counts[None, :], (slices, EXPERTS)).reshape(expert_count, 1)
    full_rows = lax.all_gather(tokens, "hidden", axis=1, tiled=True)
    row_width = full_rows.shape[1]
    bucket = jnp.dot(dispatch, full_rows, preferred_element_type=jnp.float32).astype(jnp.bfloat16)
    bucket = jnp.broadcast_to(
        bucket.reshape(1, EXPERTS, CAP, row_width), (slices, EXPERTS, CAP, row_width)
    )
    arrived = lax.all_to_all(
        bucket.reshape(expert_count, CAP, row_width),
        "expert",
        split_axis=0,
        concat_axis=0,
        tiled=True,
    )
    arrived_counts = lax.all_to_all(count_send, "expert", split_axis=0, concat_axis=0, tiled=True)
    row_width = arrived.shape[2]
    total_rows = expert_count * CAP
    flat_rows = arrived.reshape(total_rows, row_width)
    w_gate = gate_weight[0]
    w_up = up_weight[0]
    w_down = down_weight[0]
    contract = (((1,), (1,)), ((), ()))
    arrived_count = arrived_counts.reshape(expert_count).astype(jnp.int32)
    row_index = jnp.arange(total_rows, dtype=jnp.int32)
    slot_within = row_index % CAP
    is_live = slot_within < jnp.repeat(arrived_count, CAP)
    gate_pre = lax.dot_general(flat_rows, w_gate, contract, preferred_element_type=jnp.float32)
    up_pre = lax.dot_general(flat_rows, w_up, contract, preferred_element_type=jnp.float32)
    hidden = (jax.nn.silu(gate_pre) * up_pre).astype(jnp.bfloat16)
    partial_value = jnp.where(
        is_live[:, None],
        jnp.dot(hidden, w_down, preferred_element_type=jnp.float32).astype(jnp.bfloat16),
        jnp.zeros((), jnp.bfloat16),
    )
    returned = lax.all_to_all(
        partial_value.reshape(expert_count, CAP, -1),
        "expert",
        split_axis=0,
        concat_axis=0,
        tiled=True,
    )
    summed = jnp.sum(returned.reshape(slices, EXPERTS * CAP, -1).astype(jnp.float32), axis=0)
    mixed = lax.dot_general(
        weighted, summed, (((0,), (0,)), ((), ())), precision=lax.Precision.HIGHEST
    )
    result = lax.psum_scatter(mixed.astype(jnp.bfloat16), "hidden", scatter_dimension=1, tiled=True)
    return result


def solution(mesh):
    in_specs = (
        P(("groups", "expert"), "hidden"),
        P(("groups", "expert"), None),
        P(("groups", "expert"), None),
        P("expert", "hidden", None),
        P("expert", "hidden", None),
        P("expert", "hidden", None),
    )
    out_specs = P(("groups", "expert"), "hidden")
    return jax.shard_map(
        per_device, mesh=mesh, in_specs=in_specs, out_specs=out_specs, check_vma=False
    )
```

profile of v0, /device:TPU:0, one launch (start us, length us, event | category | flops | bytes accessed | tf_op | source)
XLA Modules:
  0.0 84.1 jit_solution(6986118051445558806)
XLA Ops:
  6.5 0.8 copy.14
  7.3 0.1 reshape.81
  7.4 0.1 fusion.28
  7.4 0.1 reduce_window_sum.11
  7.5 0.2 fusion.29
  7.7 0.7 copy.16
  8.4 7.3 %all-to-all-start = ((bf16[8,1,1]{2,1,0:T(2,128)(2,1)}), bf16[8,1,1]{2,1,0:T(2,128)(2,1)S(1)}, u32[]{:S(2)}, u32[]{:S(2)}) async-start(bf16[8,1,1]{2,1,0:T(2,128)(2,1)} %copy.16), calls=%async_computation | async-start | bytes 8192 | tf_op jit(solution)/shard_map/all_to_all | solution.py:47
  15.7 2.1 %all_gather.3 = bf16[8,3072]{1,0:T(8,128)(2,1)S(1)} all-gather(bf16[8,1536]{1,0:T(8,128)(2,1)} %param.6), channel_id=1, replica_groups=mesh['groups'=2,'expert'=8,'hidden'=2] {'hidden'}, dimensions={1}, use_global_device_ids=true | all-gather | bytes 73728 | tf_op jit(solution)/shard_map/all_gather | solution.py:34
  17.7 0.2 convolution_convert_fusion.2
  18.0 0.2 convolution_convert_fusion
  18.2 0.8 reshape_reshape.3
  19.0 3.1 %all-to-all-done = bf16[8,1,1]{2,1,0:T(2,128)(2,1)S(1)} async-done(((bf16[8,1,1]{2,1,0:T(2,128)(2,1)}), bf16[8,1,1]{2,1,0:T(2,128)(2,1)S(1)}, u32[]{:S(2)}, u32[]{:S(2)}) %all-to-all-start) | async-done | bytes 48 | tf_op jit(solution)/shard_map/all_to_all | solution.py:47
  22.0 3.4 %all-to-all-start.1 = ((bf16[8,4,3072]{2,1,0:T(4,128)(2,1)}), bf16[8,4,3072]{2,1,0:T(4,128)(2,1)S(1)}, u32[]{:S(2)}, u32[]{:S(2)}) async-start(bf16[8,4,3072]{2,1,0:T(4,128)(2,1)} %reshape_reshape.3), calls=%async_computation.1 | async-start | bytes 393216 | tf_op jit(solution)/shard_map/all_to_all | solution.py:40
  25.4 0.2 convert_reduce_fusion
  25.7 0.1 broadcast_in_dim.27
  25.7 0.1 reshape.82
  25.8 7.4 %all-to-all-done.1 = bf16[8,4,3072]{2,1,0:T(4,128)(2,1)S(1)} async-done(((bf16[8,4,3072]{2,1,0:T(4,128)(2,1)}), bf16[8,4,3072]{2,1,0:T(4,128)(2,1)S(1)}, u32[]{:S(2)}, u32[]{:S(2)}) %all-to-all-start.1) | async-done | bytes 196640 | tf_op jit(solution)/shard_map/all_to_all | solution.py:40
  33.3 10.6 %fusion.4 = f32[32,2688]{1,0:T(8,128)S(1)} fusion(bf16[32,3072]{1,0:T(8,128)(2,1)S(1)} %reshape.83, bf16[1,2688,3072]{2,1,0:T(8,128)(2,1)} %param.9), kind=kOutput, calls=%fused_computation.4 | convolution fusion | flops 528482304 | bytes 17055744 | tf_op jit(solution)/shard_map/dot_general | solution.py:59
  43.9 0.0 copy-start
  43.9 14.7 %fusion.15 = bf16[32,3072]{1,0:T(8,128)(2,1)S(1)} fusion(bf16[1,2688,3072]{2,1,0:T(8,128)(2,1)} %param.11, bf16[32,3072]{1,0:T(8,128)(2,1)S(1)} %reshape.83, bf16[1,2688,3072]{2,1,0:T(8,128)(2,1)} %param.10, f32[32,2688]{1,0:T(8,128)S(1)} %fusion.4, pred[32]{0:T(512)(128)(4,1)S(1)} %fusion.36), kind=kOutput, calls=%fused_computation.11 | convolution fusion | flops 1057677312 | bytes 33767456 | tf_op jit(solution)/shard_map/dot_general | solution.py:64
  58.6 0.8 reshape.84
  59.3 3.4 %all-to-all-start.2 = ((bf16[8,4,3072]{2,1,0:T(4,128)(2,1)}), bf16[8,4,3072]{2,1,0:T(4,128)(2,1)S(1)}, u32[]{:S(2)}, u32[]{:S(2)}) async-start(bf16[8,4,3072]{2,1,0:T(4,128)(2,1)} %reshape.84), calls=%async_computation.2 | async-start | bytes 393216 | tf_op jit(solution)/shard_map/all_to_all | solution.py:67
  62.7 0.0 reduce-scatter.2.cloned.1.call-start
  62.8 0.0 copy-done
  62.8 0.1 copy.15
  62.9 0.1 div.26
  62.9 0.3 fusion.26
  63.2 7.2 %all-to-all-done.2 = bf16[8,4,3072]{2,1,0:T(4,128)(2,1)S(1)} async-done(((bf16[8,4,3072]{2,1,0:T(4,128)(2,1)}), bf16[8,4,3072]{2,1,0:T(4,128)(2,1)S(1)}, u32[]{:S(2)}, u32[]{:S(2)}) %all-to-all-start.2) | async-done | bytes 196640 | tf_op jit(solution)/shard_map/all_to_all | solution.py:67
  70.5 0.8 convolution_convert_fusion.1
  71.3 0.0 reduce-scatter.2.cloned.1.call-update
  71.3 5.9 %reduce-scatter.2.cloned.1.call-done = bf16[8,1536]{1,0:T(8,128)(2,1)} async-done(((bf16[8,3072]{1,0:T(8,128)(2,1)}), bf16[8,1536]{1,0:T(8,128)(2,1)}) %reduce-scatter.2.cloned.1.call-update) | async-done | bytes 24592 | tf_op jit(solution)/shard_map/reduce_scatter | solution.py:78
  (6 shorter events, 0.1 us)
Async XLA Ops:
  8.4 13.6 %all-to-all-start = ((bf16[8,1,1]{2,1,0:T(2,128)(2,1)}), bf16[8,1,1]{2,1,0:T(2,128)(2,1)S(1)}, u32[]{:S(2)}, u32[]{:S(2)}) async-start(bf16[8,1,1]{2,1,0:T(2,128)(2,1)} %copy.16), calls=%async_computation | async-start | bytes 8192 | tf_op jit(solution)/shard_map/all_to_all | solution.py:47
  22.0 11.2 %all-to-all-start.1 = ((bf16[8,4,3072]{2,1,0:T(4,128)(2,1)}), bf16[8,4,3072]{2,1,0:T(4,128)(2,1)S(1)}, u32[]{:S(2)}, u32[]{:S(2)}) async-start(bf16[8,4,3072]{2,1,0:T(4,128)(2,1)} %reshape_reshape.3), calls=%async_computation.1 | async-start | bytes 393216 | tf_op jit(solution)/shard_map/all_to_all | solution.py:40
  43.9 18.9 %copy-start = (s32[8,4]{0,1:T(4,128)S(1)}, s32[8,4]{0,1:T(4,128)}, u32[]{:S(2)}) copy-start(s32[8,4]{0,1:T(4,128)} %param.8) | copy-start | bytes 388
  59.3 11.1 %all-to-all-start.2 = ((bf16[8,4,3072]{2,1,0:T(4,128)(2,1)}), bf16[8,4,3072]{2,1,0:T(4,128)(2,1)S(1)}, u32[]{:S(2)}, u32[]{:S(2)}) async-start(bf16[8,4,3072]{2,1,0:T(4,128)(2,1)} %reshape.84), calls=%async_computation.2 | async-start | bytes 393216 | tf_op jit(solution)/shard_map/all_to_all | solution.py:67
  62.7 14.5 %reduce-scatter.2.cloned.1.call-start = ((), (), s32[]{:S(2)}) async-start(), calls=%async_computation.4 | async-start | bytes 73728 | tf_op jit(solution)/shard_map/reduce_scatter | solution.py:78
Sparse Core Ops, SparseCore 0:
  71.5 5.7 reduce-scatter.1
where the time goes:
time: 84.5 us; the launch traced here: 84.1 us
  matrix products  26.9 us (32%)
  waiting for transfers between devices  23.6 us (28%)
  starting transfers between devices  14.1 us (17%)
  between operations  13.5 us (16%)
  local copies, waits for them, and re-layouts  3.45 us (4%)
  blocking collectives  2.05 us (2%)
    dot_general x1, matrix products, per_device(): jnp.dot(hidden, w_down, preferred_element_type=jnp.float32)  14.7 us
    dot_general x1, matrix products, per_device(): lax.dot_general(flat_rows, w_gate, contract, preferred_element_type=jnp.f...  10.6 us
    all_to_all x1, waiting for transfers between devices, per_device(): lax.all_to_all(bucket.reshape(expert_count, CAP, row_width), 'expert', sp...  7.39 us
    all_to_all x1, starting transfers between devices, per_device(): lax.all_to_all(count_send, 'expert', split_axis=0, concat_axis=0, tiled=T...  7.25 us
    all_to_all x1, waiting for transfers between devices, per_device(): lax.all_to_all(partial_value.reshape(expert_count, CAP, -1), 'expert', sp...  7.23 us
    reduce_scatter x1, waiting for transfers between devices, per_device(): lax.psum_scatter(mixed.astype(jnp.bfloat16), 'hidden', scatter_dimension=...  5.89 us
    all_to_all x1, starting transfers between devices, per_device(): lax.all_to_all(bucket.reshape(expert_count, CAP, row_width), 'expert', sp...  3.39 us
    all_to_all x1, starting transfers between devices, per_device(): lax.all_to_all(partial_value.reshape(expert_count, CAP, -1), 'expert', sp...  3.39 us
  transfers between devices with their start and end apart: 4, of which 4 were waited for; matrix products, arithmetic and copies ran while one was open for 2% of the time, Pallas kernels for 0%

commit v1 on v0

v1 whole, which is shorter than its diff:
```python
import functools

import jax
import jax.numpy as jnp
from jax import lax
from jax.experimental import pallas as pl
from jax.experimental.pallas import tpu as pltpu
from jax.sharding import PartitionSpec as P

EXPERTS = 8
CAP = 4
GROUPS = 4
BLOCK = GROUPS * CAP
COLS = 512
STEP = 512
MESH = pl.DeviceIdType.MESH


def hidden_steps(units):
    return [(at, min(STEP, units - at)) for at in range(0, units, STEP)]


def iota(shape, axis):
    return lax.broadcasted_iota(jnp.int32, shape, axis)


def moe_kernel(
    n, tok_ref, ids_ref, codes_ref, gate_hbm, up_hbm, down_hbm, out_ref,
    w_gate, w_up, w_down, send_rows, got_rows, rows, hidden, send_out, got_out,
    gate_sem, up_sem, down_sem, rows_sent, rows_got, out_sent, out_got,
):
    tok_dev, half = tok_ref.shape
    units, width = gate_hbm.shape[1:]
    steps = hidden_steps(units)
    per_half = half // COLS
    order = [part * per_half + at for at in range(per_half) for part in range(2)]
    group = lax.axis_index("groups")
    me = lax.axis_index("expert")
    core = lax.axis_index("hidden")

    gate_copy = [
        pltpu.make_async_copy(
            gate_hbm.at[0, pl.ds(at, size)], w_gate.at[pl.ds(at, size)], gate_sem.at[j]
        )
        for j, (at, size) in enumerate(steps)
    ]
    up_copy = [
        pltpu.make_async_copy(
            up_hbm.at[0, pl.ds(at, size)], w_up.at[pl.ds(at, size)], up_sem.at[j]
        )
        for j, (at, size) in enumerate(steps)
    ]
    down_copy = {
        c: pltpu.make_async_copy(
            down_hbm.at[0, :, pl.ds(c * COLS, COLS)], w_down.at[c], down_sem.at[c]
        )
        for c in order
    }
    for j in range(len(steps)):
        gate_copy[j].start()
        up_copy[j].start()
    for c in order:
        down_copy[c].start()

    barrier = pltpu.get_barrier_semaphore()

    @pl.loop(1, n)
    def _(k):
        other = lax.rem(me + k, n)
        for part in range(2):
            pl.semaphore_signal(
                barrier, inc=1, device_id=(group, other, part), device_id_type=MESH
            )

    pl.semaphore_signal(barrier, inc=1, device_id=(group, me, 1 - core), device_id_type=MESH)

    stacked = GROUPS * tok_dev
    slots = (stacked, EXPERTS * BLOCK)
    row, col = iota(slots, 0), iota(slots, 1)
    ids = jnp.concatenate([ids_ref[...]] * GROUPS, axis=0)
    codes = jnp.concatenate([codes_ref[...]] * GROUPS, axis=0)
    named = jnp.zeros(slots, jnp.bool_)
    code = jnp.zeros(slots, jnp.int32)
    for k in range(ids.shape[1]):
        same = ids[:, k:k + 1] == col // BLOCK
        named = named | same
        code = code + jnp.where(same, codes[:, k:k + 1], 0)
    square = (stacked, stacked)
    a, b = iota(square, 0), iota(square, 1)
    earlier = (a // tok_dev == b // tok_dev) & (b < a)
    place = jnp.dot(
        earlier.astype(jnp.float32).astype(jnp.bfloat16),
        named.astype(jnp.float32).astype(jnp.bfloat16),
        preferred_element_type=jnp.float32,
    ).astype(jnp.int32)
    hit = named & (place == col % CAP) & ((col // CAP) % GROUPS == row // tok_dev)
    pick = hit.astype(jnp.float32)
    high = pick * (code // 256).astype(jnp.float32) / 128.0
    low = pick * (code % 256).astype(jnp.float32) / 32768.0
    gains = jnp.concatenate([high, low], axis=0).astype(jnp.bfloat16)

    tok = tok_ref[...].astype(jnp.float32)
    piece = half // GROUPS
    tall = jnp.concatenate(
        [tok[:, g * piece:(g + 1) * piece] for g in range(GROUPS)], axis=0
    ).astype(jnp.bfloat16)
    send_rows[...] = (
        lax.dot_general(
            pick.T.astype(jnp.bfloat16), tall, (((1,), (0,)), ((), ())),
            preferred_element_type=jnp.float32,
        )
        .astype(jnp.bfloat16)
        .reshape(EXPERTS, BLOCK, piece)
    )

    pl.semaphore_wait(barrier, 2 * n - 1)

    def rows_to(other, part):
        return pltpu.make_async_remote_copy(
            src_ref=send_rows.at[lax.rem(other, EXPERTS)],
            dst_ref=got_rows.at[core * n + me],
            send_sem=rows_sent,
            recv_sem=rows_got,
            device_id=(group, other, part),
            device_id_type=MESH,
        )

    @pl.loop(1, n)
    def _(k):
        other = lax.rem(me + k, n)
        for part in range(2):
            rows_to(other, part).start()

    rows_to(me, 1 - core).start()
    pltpu.make_async_copy(
        send_rows.at[lax.rem(me, EXPERTS)], got_rows.at[core * n + me], rows_got
    ).start()

    flat = EXPERTS * BLOCK
    lot = EXPERTS * CAP
    a, b = iota((flat, flat), 0), iota((flat, flat), 1)
    split = (a // lot) == (b // CAP) % GROUPS
    split = split & ((a % lot) // CAP == b // BLOCK) & (a % CAP == b % CAP)
    split = split.astype(jnp.float32).astype(jnp.bfloat16)
    join = (b // lot) == (a // CAP) % GROUPS
    join = join & ((b % lot) // CAP == a // BLOCK) & (b % CAP == a % CAP)
    join = join.astype(jnp.float32).astype(jnp.bfloat16)

    pltpu.make_async_copy(got_rows, got_rows, rows_got).wait()
    for s in range(n // EXPERTS):
        for part in range(2):
            block = got_rows[part * n + s * EXPERTS:part * n + (s + 1) * EXPERTS]
            block = jnp.dot(
                split, block.reshape(flat, piece), preferred_element_type=jnp.float32
            ).astype(jnp.bfloat16)
            for g in range(GROUPS):
                at = part * half + g * piece
                rows[s * lot:(s + 1) * lot, at:at + piece] = block[g * lot:(g + 1) * lot]

    contract = (((1,), (1,)), ((), ()))
    for j, (at, size) in enumerate(steps):
        gate_copy[j].wait()
        gate_pre = lax.dot_general(
            rows[...], w_gate[at:at + size], contract, preferred_element_type=jnp.float32
        )
        up_copy[j].wait()
        up_pre = lax.dot_general(
            rows[...], w_up[at:at + size], contract, preferred_element_type=jnp.float32
        )
        silu = gate_pre / (1.0 + jnp.exp(-gate_pre))
        hidden[:, at:at + size] = (silu * up_pre).astype(jnp.bfloat16)

    lane = COLS // GROUPS
    for c in order:
        part, at = c // per_half, c % per_half
        down_copy[c].wait()
        out = jnp.dot(hidden[...], w_down[c], preferred_element_type=jnp.float32)
        out = out.astype(jnp.bfloat16)
        for s in range(n // EXPERTS):
            block = jnp.concatenate(
                [
                    out[s * lot:(s + 1) * lot, g * lane:(g + 1) * lane]
                    for g in range(GROUPS)
                ],
                axis=0,
            )
            send_out[c, s * EXPERTS:(s + 1) * EXPERTS] = (
                jnp.dot(join, block, preferred_element_type=jnp.float32)
                .astype(jnp.bfloat16)
                .reshape(EXPERTS, BLOCK, lane)
            )

        def out_to(other):
            return pltpu.make_async_remote_copy(
                src_ref=send_out.at[c, other],
                dst_ref=got_out.at[(at * 2 + core) * n + me],
                send_sem=out_sent,
                recv_sem=out_got.at[at],
                device_id=(group, other, part),
                device_id_type=MESH,
            )

        @pl.loop(1, n)
        def _(k):
            out_to(lax.rem(me + k, n)).start()

        @pl.when(core == part)
        def _():
            pltpu.make_async_copy(
                send_out.at[c, me], got_out.at[(at * 2 + core) * n + me], out_got.at[at]
            ).start()

        @pl.when(core != part)
        def _():
            out_to(me).start()

    for at in range(per_half):
        landed = got_out.at[pl.ds(at * 2 * n, 2 * n)]
        pltpu.make_async_copy(landed, landed, out_got.at[at]).wait()
        total = jnp.zeros((2 * stacked, lane), jnp.float32)
        for s in range(2 * n // EXPERTS):
            first = at * 2 * n + s * EXPERTS
            block = got_out[first:first + EXPERTS].reshape(flat, lane)
            total = total + jnp.dot(gains, block, preferred_element_type=jnp.float32)
        mixed = total[:stacked] + total[stacked:]
        for g in range(GROUPS):
            to = at * COLS + g * lane
            out_ref[:, to:to + lane] = mixed[g * tok_dev:(g + 1) * tok_dev].astype(
                out_ref.dtype
            )

    sent = got_rows.at[pl.ds(0, 2 * n - 1)]
    pltpu.make_async_copy(sent, sent, rows_sent).wait()
    sent = got_out.at[pl.ds(0, 2 * per_half * n - per_half)]
    pltpu.make_async_copy(sent, sent, out_sent).wait()


def per_device(tokens, expert_ids, gate_codes, gate_weight, up_weight, down_weight):
    n = lax.axis_size("expert")
    tok_dev, half = tokens.shape
    units, width = gate_weight.shape[1:]
    parts = len(hidden_steps(units))
    columns = width // COLS
    piece = half // GROUPS
    bf16 = jnp.bfloat16
    return pl.pallas_call(
        functools.partial(moe_kernel, n),
        out_shape=jax.ShapeDtypeStruct((tok_dev, half), bf16),
        in_specs=[pl.BlockSpec(memory_space=pltpu.VMEM)] * 3
        + [pl.BlockSpec(memory_space=pl.ANY)] * 3,
        out_specs=pl.BlockSpec(memory_space=pltpu.VMEM),
        scratch_shapes=[
            pltpu.VMEM((units, width), bf16),
            pltpu.VMEM((units, width), bf16),
            pltpu.VMEM((columns, units, COLS), bf16),
            pltpu.VMEM((EXPERTS, BLOCK, piece), bf16),
            pltpu.VMEM((2 * n, BLOCK, piece), bf16),
            pltpu.VMEM((n * CAP, width), bf16),
            pltpu.VMEM((n * CAP, units), bf16),
            pltpu.VMEM((columns, n, BLOCK, COLS // GROUPS), bf16),
            pltpu.VMEM((columns * n, BLOCK, COLS // GROUPS), bf16),
            pltpu.SemaphoreType.DMA((parts,)),
            pltpu.SemaphoreType.DMA((parts,)),
            pltpu.SemaphoreType.DMA((columns,)),
            pltpu.SemaphoreType.DMA,
            pltpu.SemaphoreType.DMA,
            pltpu.SemaphoreType.DMA,
            pltpu.SemaphoreType.DMA((half // COLS,)),
        ],
        compiler_params=pltpu.CompilerParams(
            collective_id=0, has_side_effects=True, vmem_limit_bytes=58 * 1024 * 1024
        ),
    )(tokens, expert_ids, gate_codes, gate_weight, up_weight, down_weight)


def solution(mesh):
    in_specs = (
        P(("groups", "expert"), "hidden"),
        P(("groups", "expert"), None),
        P(("groups", "expert"), None),
        P("expert", "hidden", None),
        P("expert", "hidden", None),
        P("expert", "hidden", None),
    )
    out_specs = P(("groups", "expert"), "hidden")
    return jax.shard_map(
        per_device, mesh=mesh, in_specs=in_specs, out_specs=out_specs, check_vma=False
    )
```

time: 84.5 us -> 38.4 us (0.45)
  Pallas kernels: 0 us -> 33.9 us
  matrix products: 26.9 us -> 0 us
  waiting for transfers between devices: 23.6 us -> 0 us
  starting transfers between devices: 14.1 us -> 0 us
  between operations: 13.5 us -> 0.01 us
  blocking collectives: 2.05 us -> 0 us
    pallas_call x0 -> x1, Pallas kernels: none -> 33.9 us  [per_device(): pl.pallas_call(functools.partial(moe_kernel, n), out_shape=jax.ShapeDtype...]
    dot_general x6 -> x0, matrix products: 26.9 us -> none  [the longest x1 14.7 us: per_device(): jnp.dot(hidden, w_down, preferred_element_type=jnp.float32)]
    all_to_all x3 -> x0, waiting for transfers between devices: 17.7 us -> none  [the longest x1 7.39 us: per_device(): lax.all_to_all(bucket.reshape(expert_count, CAP, row_width), 'expert', sp...]
    all_to_all x3 -> x0, starting transfers between devices: 14 us -> none  [the longest x1 7.25 us: per_device(): lax.all_to_all(count_send, 'expert', split_axis=0, concat_axis=0, tiled=T...]
    reduce_scatter x1 -> x0, waiting for transfers between devices: 5.89 us -> none  [per_device(): lax.psum_scatter(mixed.astype(jnp.bfloat16), 'hidden', scatter_dimension=...]
    unnamed x3, local copies, waits for them, and re-layouts: 0.76 us -> 4.04 us
    all_gather x1 -> x0, blocking collectives: 2.05 us -> none  [per_device(): full_rows = lax.all_gather(tokens, 'hidden', axis=1, tiled=True)]
    reshape x4 -> x0, local copies, waits for them, and re-layouts: 0.96 us -> none  [the longest x1 0.75 us: per_device(): partial_value.reshape(expert_count, CAP, -1)]
  transfers between devices with their start and end apart: 4 -> 0, of which waited for: 4 -> 0; matrix products, arithmetic and copies ran while one was open for 2% -> 0% of each run, Pallas kernels for 0% -> 0%
where the time goes in v1:
time: 38.4 us; the launch traced here: 38 us
  Pallas kernels  33.9 us (88%)
  local copies, waits for them, and re-layouts  4.04 us (11%)
    pallas_call x1, Pallas kernels, per_device(): pl.pallas_call(functools.partial(moe_kernel, n), out_shape=jax.ShapeDtype...  33.9 us
    unnamed x3, local copies, waits for them, and re-layouts  4.04 us

profile of v1, /device:TPU:0, one launch (start us, length us, event | category | flops | bytes accessed | tf_op | source)
XLA Modules:
  0.0 38.0 jit_solution(7484078453037174683)
XLA Ops:
  0.0 1.3 %copy.7.ids_ref = s32[8,4]{1,0:T(8,128)} copy(s32[8,4]{0,1:T(4,128)} %param.7) | data formatting | bytes 256 | tf_op args[1]
  1.3 1.3 %copy.8.codes_ref = s32[8,4]{1,0:T(8,128)} copy(s32[8,4]{0,1:T(4,128)} %param.8) | data formatting | bytes 256 | tf_op args[2]
  2.7 33.9 %shard_map.64 = bf16[8,1536]{1,0:T(8,128)(2,1)} custom-call(bf16[8,1536]{1,0:T(8,128)(2,1)} %tok_ref.1, s32[8,4]{1,0:T(8,128)} %copy.7.ids_ref, s32[8,4]{1,0:T(8,128)} %copy.8.codes_ref, bf16[1,2688,3072]{2,1,0:T(8,128)(2,1)} %gate_hbm.1, bf16[1,2688,3072]{2,1,0:T(8,128)(2,1)} %up_hbm.1, bf16[1,2688,3072]{2,1,0:T(8,128)(2,1)} %down_hbm.1), custom_call_target="tpu_custom_call" | custom-call | tf_op jit(solution)/shard_map/pallas_call | solution.py:246
  36.6 1.3 %copy.10 = bf16[8,1536]{1,0:T(8,128)(2,1)} copy(bf16[8,1536]{1,0:T(8,128)(2,1)} %shard_map.64) | data formatting | bytes 49152

commit v2 on v1

v2 whole, which is shorter than its diff:
```python
import functools

import jax
import jax.numpy as jnp
from jax import lax
from jax.experimental import pallas as pl
from jax.experimental.pallas import tpu as pltpu
from jax.sharding import PartitionSpec as P

EXPERTS = 8
CAP = 4
GROUPS = 4
BLOCK = GROUPS * CAP
COLS = 512
STEP = 512
MESH = pl.DeviceIdType.MESH


def hidden_steps(units):
    return [(at, min(STEP, units - at)) for at in range(0, units, STEP)]


def iota(shape, axis):
    return lax.broadcasted_iota(jnp.int32, shape, axis)


def moe_kernel(
    n, tok_ref, ids_ref, codes_ref, gate_hbm, up_hbm, down_hbm, out_ref,
    w_gate, w_up, w_down, send_rows, got_rows, rows, hidden, send_out, pair_out,
    got_out, gate_sem, up_sem, down_sem, rows_sent, rows_got, share_sem, pair_sem, out_sent,
    out_got,
):
    tok_dev, half = tok_ref.shape
    units, width = gate_hbm.shape[1:]
    steps = hidden_steps(units)
    per_half = half // COLS
    group = lax.axis_index("groups")
    me = lax.axis_index("expert")
    core = lax.axis_index("hidden")

    column = [pl.multiple_of(core * half, half), pl.multiple_of((1 - core) * half, half)]

    def fetch(source, target, sems, j, side):
        at, size = steps[j]
        return pltpu.make_async_copy(
            source.at[0, pl.ds(at, size), pl.ds(column[side], half)],
            target.at[side, pl.ds(at, size)],
            sems.at[side, j],
        )

    gate_copy = [[fetch(gate_hbm, w_gate, gate_sem, j, i) for i in range(2)] for j in range(len(steps))]
    up_copy = [[fetch(up_hbm, w_up, up_sem, j, i) for i in range(2)] for j in range(len(steps))]
    down_copy = [
        pltpu.make_async_copy(
            down_hbm.at[
                0, :, pl.ds(pl.multiple_of(column[1 - c // per_half] + c % per_half * COLS, COLS), COLS)
            ],
            w_down.at[c],
            down_sem.at[c],
        )
        for c in range(2 * per_half)
    ]
    for j in range(len(steps)):
        for side in range(2):
            gate_copy[j][side].start()
            up_copy[j][side].start()
    for copy in down_copy:
        copy.start()

    barrier = pltpu.get_barrier_semaphore()

    @pl.loop(1, n)
    def _(k):
        other = lax.rem(me + k, n)
        pl.semaphore_signal(barrier, inc=1, device_id=(group, other, core), device_id_type=MESH)

    pl.semaphore_signal(barrier, inc=1, device_id=(group, me, 1 - core), device_id_type=MESH)

    stacked = GROUPS * tok_dev
    slots = (stacked, EXPERTS * BLOCK)
    row, col = iota(slots, 0), iota(slots, 1)
    ids = jnp.concatenate([ids_ref[...].T] * GROUPS, axis=0)
    codes = jnp.concatenate([codes_ref[...].T] * GROUPS, axis=0)
    named = jnp.zeros(slots, jnp.bool_)
    code = jnp.zeros(slots, jnp.int32)
    for k in range(ids.shape[1]):
        same = ids[:, k:k + 1] == col // BLOCK
        named = named | same
        code = code + jnp.where(same, codes[:, k:k + 1], 0)
    square = (stacked, stacked)
    a, b = iota(square, 0), iota(square, 1)
    earlier = (a // tok_dev == b // tok_dev) & (b < a)
    place = jnp.dot(
        earlier.astype(jnp.float32).astype(jnp.bfloat16),
        named.astype(jnp.float32).astype(jnp.bfloat16),
        preferred_element_type=jnp.float32,
    ).astype(jnp.int32)
    hit = named & (place == col % CAP) & ((col // CAP) % GROUPS == row // tok_dev)
    pick = hit.astype(jnp.float32)
    high = pick * (code // 256).astype(jnp.float32) / 128.0
    low = pick * (code % 256).astype(jnp.float32) / 32768.0
    gains = jnp.concatenate([high, low], axis=0).astype(jnp.bfloat16)

    tok = tok_ref[...].astype(jnp.float32)
    piece = half // GROUPS
    tall = jnp.concatenate(
        [tok[:, g * piece:(g + 1) * piece] for g in range(GROUPS)], axis=0
    ).astype(jnp.bfloat16)
    send_rows[...] = (
        lax.dot_general(
            pick.T.astype(jnp.bfloat16), tall, (((1,), (0,)), ((), ())),
            preferred_element_type=jnp.float32,
        )
        .astype(jnp.bfloat16)
        .reshape(EXPERTS, BLOCK, piece)
    )

    pl.semaphore_wait(barrier, n)

    @pl.loop(1, n)
    def _(k):
        other = lax.rem(me + k, n)
        pltpu.make_async_remote_copy(
            src_ref=send_rows.at[lax.rem(other, EXPERTS)],
            dst_ref=got_rows.at[0, me],
            send_sem=rows_sent,
            recv_sem=rows_got,
            device_id=(group, other, core),
            device_id_type=MESH,
        ).start()

    pltpu.make_async_copy(
        send_rows.at[lax.rem(me, EXPERTS)], got_rows.at[0, me], rows_got
    ).start()

    flat = EXPERTS * BLOCK
    lot = EXPERTS * CAP
    a, b = iota((flat, flat), 0), iota((flat, flat), 1)
    split = (a // lot) == (b // CAP) % GROUPS
    split = split & ((a % lot) // CAP == b // BLOCK) & (a % CAP == b % CAP)
    split = split.astype(jnp.float32).astype(jnp.bfloat16)
    join = (b // lot) == (a // CAP) % GROUPS
    join = join & ((b % lot) // CAP == a // BLOCK) & (b % CAP == a % CAP)
    join = join.astype(jnp.float32).astype(jnp.bfloat16)

    pltpu.make_async_copy(got_rows.at[0], got_rows.at[0], rows_got).wait()
    share = pltpu.make_async_remote_copy(
        src_ref=got_rows.at[0],
        dst_ref=got_rows.at[1],
        send_sem=share_sem.at[0],
        recv_sem=share_sem.at[1],
        device_id=(group, me, 1 - core),
        device_id_type=MESH,
    )
    share.start()

    def place_rows(side):
        for s in range(n // EXPERTS):
            block = got_rows[side, s * EXPERTS:(s + 1) * EXPERTS]
            block = jnp.dot(
                split, block.reshape(flat, piece), preferred_element_type=jnp.float32
            ).astype(jnp.bfloat16)
            for g in range(GROUPS):
                rows[side, s * lot:(s + 1) * lot, g * piece:(g + 1) * piece] = block[
                    g * lot:(g + 1) * lot
                ]

    def project(copies, weight, j, side):
        at, size = steps[j]
        copies[j][side].wait()
        return lax.dot_general(
            rows[side], weight[side, at:at + size], (((1,), (1,)), ((), ())),
            preferred_element_type=jnp.float32,
        )

    place_rows(0)
    for j, (at, size) in enumerate(steps):
        gate_pre = project(gate_copy, w_gate, j, 0)
        up_pre = project(up_copy, w_up, j, 0)
        if j == 0:
            share.wait()
            place_rows(1)
        gate_pre = gate_pre + project(gate_copy, w_gate, j, 1)
        up_pre = up_pre + project(up_copy, w_up, j, 1)
        silu = gate_pre / (1.0 + jnp.exp(-gate_pre))
        hidden[:, at:at + size] = (silu * up_pre).astype(jnp.bfloat16)

    lane = COLS // GROUPS
    pair = [
        pltpu.make_async_remote_copy(
            src_ref=send_out.at[c],
            dst_ref=pair_out.at[c],
            send_sem=pair_sem.at[0, c],
            recv_sem=pair_sem.at[1, c],
            device_id=(group, me, 1 - core),
            device_id_type=MESH,
        )
        for c in range(per_half)
    ]
    for c in range(2 * per_half):
        at = c % per_half
        down_copy[c].wait()
        out = jnp.dot(hidden[...], w_down[c], preferred_element_type=jnp.float32)
        out = out.astype(jnp.bfloat16)
        if c >= per_half:
            pair[at].wait_recv()
        for s in range(n // EXPERTS):
            span = slice(s * EXPERTS, (s + 1) * EXPERTS)
            block = jnp.concatenate(
                [
                    out[s * lot:(s + 1) * lot, g * lane:(g + 1) * lane]
                    for g in range(GROUPS)
                ],
                axis=0,
            )
            block = jnp.dot(join, block, preferred_element_type=jnp.float32)
            if c >= per_half:
                block = block + pair_out[at, span].reshape(flat, lane).astype(jnp.float32)
            send_out[c, span] = block.astype(jnp.bfloat16).reshape(EXPERTS, BLOCK, lane)
        if c < per_half:
            pair[c].start()
        else:

            @pl.loop(1, n)
            def _(k):
                other = lax.rem(me + k, n)
                pltpu.make_async_remote_copy(
                    src_ref=send_out.at[c, other],
                    dst_ref=got_out.at[at, me],
                    send_sem=out_sent.at[at],
                    recv_sem=out_got.at[at],
                    device_id=(group, other, core),
                    device_id_type=MESH,
                ).start()

            pltpu.make_async_copy(
                send_out.at[c, me], got_out.at[at, me], out_got.at[at]
            ).start()

    for at in range(per_half):
        landed = got_out.at[at]
        pltpu.make_async_copy(landed, landed, out_got.at[at]).wait()
        total = jnp.zeros((2 * stacked, lane), jnp.float32)
        for s in range(n // EXPERTS):
            block = got_out[at, s * EXPERTS:(s + 1) * EXPERTS].reshape(flat, lane)
            total = total + jnp.dot(gains, block, preferred_element_type=jnp.float32)
        mixed = total[:stacked] + total[stacked:]
        for g in range(GROUPS):
            to = at * COLS + g * lane
            out_ref[:, to:to + lane] = mixed[g * tok_dev:(g + 1) * tok_dev].astype(
                out_ref.dtype
            )

    for copy in pair:
        copy.wait_send()
    sent = got_rows.at[0, pl.ds(0, n - 1)]
    pltpu.make_async_copy(sent, sent, rows_sent).wait()
    for at in range(per_half):
        sent = got_out.at[at, pl.ds(0, n - 1)]
        pltpu.make_async_copy(sent, sent, out_sent.at[at]).wait()


def per_device(tokens, expert_ids, gate_codes, gate_weight, up_weight, down_weight):
    n = lax.axis_size("expert")
    tok_dev, half = tokens.shape
    units, width = gate_weight.shape[1:]
    parts = len(hidden_steps(units))
    columns = width // COLS
    lane = COLS // GROUPS
    piece = half // GROUPS
    bf16 = jnp.bfloat16
    return pl.pallas_call(
        functools.partial(moe_kernel, n),
        out_shape=jax.ShapeDtypeStruct((tok_dev, half), bf16),
        in_specs=[pl.BlockSpec(memory_space=pltpu.VMEM)] * 3
        + [pl.BlockSpec(memory_space=pl.ANY)] * 3,
        out_specs=pl.BlockSpec(memory_space=pltpu.VMEM),
        scratch_shapes=[
            pltpu.VMEM((2, units, half), bf16),
            pltpu.VMEM((2, units, half), bf16),
            pltpu.VMEM((columns, units, COLS), bf16),
            pltpu.VMEM((EXPERTS, BLOCK, piece), bf16),
            pltpu.VMEM((2, n, BLOCK, piece), bf16),
            pltpu.VMEM((2, n * CAP, half), bf16),
            pltpu.VMEM((n * CAP, units), bf16),
            pltpu.VMEM((columns, n, BLOCK, lane), bf16),
            pltpu.VMEM((half // COLS, n, BLOCK, lane), bf16),
            pltpu.VMEM((half // COLS, n, BLOCK, lane), bf16),
            pltpu.SemaphoreType.DMA((2, parts)),
            pltpu.SemaphoreType.DMA((2, parts)),
            pltpu.SemaphoreType.DMA((columns,)),
            pltpu.SemaphoreType.DMA,
            pltpu.SemaphoreType.DMA,
            pltpu.SemaphoreType.DMA((2,)),
            pltpu.SemaphoreType.DMA((2, half // COLS)),
            pltpu.SemaphoreType.DMA((half // COLS,)),
            pltpu.SemaphoreType.DMA((half // COLS,)),
        ],
        compiler_params=pltpu.CompilerParams(
            collective_id=0, has_side_effects=True, vmem_limit_bytes=58 * 1024 * 1024
        ),
    )(tokens, expert_ids.T, gate_codes.T, gate_weight, up_weight, down_weight)


def solution(mesh):
    in_specs = (
        P(("groups", "expert"), "hidden"),
        P(("groups", "expert"), None),
        P(("groups", "expert"), None),
        P("expert", "hidden", None),
        P("expert", "hidden", None),
        P("expert", "hidden", None),
    )
    out_specs = P(("groups", "expert"), "hidden")
    return jax.shard_map(
        per_device, mesh=mesh, in_specs=in_specs, out_specs=out_specs, check_vma=False
    )
```

time: 38.4 us -> 36.1 us (0.940)
  local copies, waits for them, and re-layouts: 4.04 us -> 1.35 us
  Pallas kernels: 33.9 us -> 34.5 us
    unnamed x3 -> x1, local copies, waits for them, and re-layouts: 4.04 us -> 1.35 us
    pallas_call x1, Pallas kernels: 33.9 us -> 34.5 us  [per_device(): pl.pallas_call(functools.partial(moe_kernel, n), out_shape=jax.ShapeDtype...]
where the time goes in v2:
time: 36.1 us; the launch traced here: 35.8 us
  Pallas kernels  34.5 us (96%)
  local copies, waits for them, and re-layouts  1.35 us (4%)
    pallas_call x1, Pallas kernels, per_device(): pl.pallas_call(functools.partial(moe_kernel, n), out_shape=jax.ShapeDtype...  34.5 us
    unnamed x1, local copies, waits for them, and re-layouts  1.35 us

profile of v2, /device:TPU:0, one launch (start us, length us, event | category | flops | bytes accessed | tf_op | source)
XLA Modules:
  0.0 35.8 jit_solution(5388394292601913630)
XLA Ops:
  0.0 34.5 %shard_map.64 = bf16[8,1536]{1,0:T(8,128)(2,1)} custom-call(bf16[8,1536]{1,0:T(8,128)(2,1)} %tok_ref.1, s32[4,8]{1,0:T(4,128)} %bitcast.2, s32[4,8]{1,0:T(4,128)} %bitcast.3, bf16[1,2688,3072]{2,1,0:T(8,128)(2,1)} %gate_hbm.1, bf16[1,2688,3072]{2,1,0:T(8,128)(2,1)} %up_hbm.1, bf16[1,2688,3072]{2,1,0:T(8,128)(2,1)} %down_hbm.1), custom_call_target="tpu_custom_call" | custom-call | tf_op jit(solution)/shard_map/pallas_call | solution.py:272
  34.5 1.3 %copy.8 = bf16[8,1536]{1,0:T(8,128)(2,1)} copy(bf16[8,1536]{1,0:T(8,128)(2,1)} %shard_map.64) | data formatting | bytes 49152

commit v3 on v2

--- a/solution.py
+++ b/solution.py
@@ -12,7 +12,7 @@
 GROUPS = 4
 BLOCK = GROUPS * CAP
 COLS = 512
-STEP = 512
+STEP = 896
 MESH = pl.DeviceIdType.MESH
 
 
@@ -38,6 +38,15 @@
     me = lax.axis_index("expert")
     core = lax.axis_index("hidden")
 
+    barrier = pltpu.get_barrier_semaphore()
+
+    @pl.loop(1, n)
+    def _(k):
+        other = lax.rem(me + k, n)
+        pl.semaphore_signal(barrier, inc=1, device_id=(group, other, core), device_id_type=MESH)
+
+    pl.semaphore_signal(barrier, inc=1, device_id=(group, me, 1 - core), device_id_type=MESH)
+
     column = [pl.multiple_of(core * half, half), pl.multiple_of((1 - core) * half, half)]
 
     def fetch(source, target, sems, j, side):
@@ -60,21 +69,14 @@
         )
         for c in range(2 * per_half)
     ]
-    for j in range(len(steps)):
-        for side in range(2):
-            gate_copy[j][side].start()
-            up_copy[j][side].start()
-    for copy in down_copy:
-        copy.start()
-
-    barrier = pltpu.get_barrier_semaphore()
-
-    @pl.loop(1, n)
-    def _(k):
-        other = lax.rem(me + k, n)
-        pl.semaphore_signal(barrier, inc=1, device_id=(group, other, core), device_id_type=MESH)
-
-    pl.semaphore_signal(barrier, inc=1, device_id=(group, me, 1 - core), device_id_type=MESH)
+    def start_weights(some):
+        for j in some:
+            for side in range(2):
+                gate_copy[j][side].start()
+                up_copy[j][side].start()
+
+    early = min(2, len(steps))
+    start_weights(range(early))
 
     stacked = GROUPS * tok_dev
     slots = (stacked, EXPERTS * BLOCK)
@@ -132,6 +134,10 @@
     pltpu.make_async_copy(
         send_rows.at[lax.rem(me, EXPERTS)], got_rows.at[0, me], rows_got
     ).start()
+
+    start_weights(range(early, len(steps)))
+    for copy in down_copy:
+        copy.start()
 
     flat = EXPERTS * BLOCK
     lot = EXPERTS * CAP

time: 36.1 us -> 35.8 us (level)
  no operation moved by 1% of the time
where the time goes in v3:
time: 35.8 us; the launch traced here: 35.6 us
  Pallas kernels  34.3 us (96%)
  local copies, waits for them, and re-layouts  1.35 us (4%)
    pallas_call x1, Pallas kernels, per_device(): pl.pallas_call(functools.partial(moe_kernel, n), out_shape=jax.ShapeDtype...  34.3 us
    unnamed x1, local copies, waits for them, and re-layouts  1.35 us

profile of v3, /device:TPU:0, one launch (start us, length us, event | category | flops | bytes accessed | tf_op | source)
XLA Modules:
  0.0 35.6 jit_solution(2076177716066475069)
XLA Ops:
  0.0 34.3 %shard_map.64 = bf16[8,1536]{1,0:T(8,128)(2,1)} custom-call(bf16[8,1536]{1,0:T(8,128)(2,1)} %tok_ref.1, s32[4,8]{1,0:T(4,128)} %bitcast.2, s32[4,8]{1,0:T(4,128)} %bitcast.3, bf16[1,2688,3072]{2,1,0:T(8,128)(2,1)} %gate_hbm.1, bf16[1,2688,3072]{2,1,0:T(8,128)(2,1)} %up_hbm.1, bf16[1,2688,3072]{2,1,0:T(8,128)(2,1)} %down_hbm.1), custom_call_target="tpu_custom_call" | custom-call | tf_op jit(solution)/shard_map/pallas_call | solution.py:278
  34.3 1.3 %copy.8 = bf16[8,1536]{1,0:T(8,128)(2,1)} copy(bf16[8,1536]{1,0:T(8,128)(2,1)} %shard_map.64) | data formatting | bytes 49152

commit v4 on v3

--- a/solution.py
+++ b/solution.py
@@ -11,7 +11,7 @@
 CAP = 4
 GROUPS = 4
 BLOCK = GROUPS * CAP
-COLS = 512
+COLS = 1536
 STEP = 896
 MESH = pl.DeviceIdType.MESH
 

time: 35.8 us -> 34.7 us (0.969)
  Pallas kernels: 34.3 us -> 33.2 us
    pallas_call x1, Pallas kernels: 34.3 us -> 33.2 us  [per_device(): pl.pallas_call(functools.partial(moe_kernel, n), out_shape=jax.ShapeDtype...]
where the time goes in v4:
time: 34.7 us; the launch traced here: 34.5 us
  Pallas kernels  33.2 us (96%)
  local copies, waits for them, and re-layouts  1.35 us (4%)
    pallas_call x1, Pallas kernels, per_device(): pl.pallas_call(functools.partial(moe_kernel, n), out_shape=jax.ShapeDtype...  33.2 us
    unnamed x1, local copies, waits for them, and re-layouts  1.35 us

profile of v4, /device:TPU:0, one launch (start us, length us, event | category | flops | bytes accessed | tf_op | source)
XLA Modules:
  0.0 34.5 jit_solution(6750526686722181801)
XLA Ops:
  0.0 33.2 %shard_map.64 = bf16[8,1536]{1,0:T(8,128)(2,1)} custom-call(bf16[8,1536]{1,0:T(8,128)(2,1)} %tok_ref.1, s32[4,8]{1,0:T(4,128)} %bitcast.2, s32[4,8]{1,0:T(4,128)} %bitcast.3, bf16[1,2688,3072]{2,1,0:T(8,128)(2,1)} %gate_hbm.1, bf16[1,2688,3072]{2,1,0:T(8,128)(2,1)} %up_hbm.1, bf16[1,2688,3072]{2,1,0:T(8,128)(2,1)} %down_hbm.1), custom_call_target="tpu_custom_call" | custom-call | tf_op jit(solution)/shard_map/pallas_call | solution.py:278
  33.2 1.3 %copy.8 = bf16[8,1536]{1,0:T(8,128)(2,1)} copy(bf16[8,1536]{1,0:T(8,128)(2,1)} %shard_map.64) | data formatting | bytes 49152
